TPU v7x, 32 devices: a whole 2x2x4 slice. The times are simulated.
32 devices in a mesh: rep: 8 (over z, y), slab: 4 (over x, core).
Axes of the slice: x: 2, y: 2, z: 4, core: 2. Of those that a mesh axis runs over, the one named last changes fastest.
Arguments:
- replica_field: float32 [16, 64, 128, 128], P('rep', 'slab')
- momentum: float32 [16, 64, 128, 128], P('rep', 'slab'), may hold values from -5 to 5
- parent: int32 [16], replicated, may hold values from 0 to 15, as said below
Outputs:
- field_out: float32 [16, 64, 128, 128], P('rep', 'slab')
- momentum_out: float32 [16, 64, 128, 128], P('rep', 'slab')
- action_density: float32 [16], P('rep')
Inputs may be any that keep to these rules, and one draw needn't show every extreme that they name: `parent`: exactly 4 entries differ from their own index, at most one among each aligned block of 2 entries; every entry that differs names an index whose own entry equals it.
All inputs are finite; a program needn't handle non-finite values.
Results may differ from a plain program's by a relative error of at most 0.00002.
Values sent between devices are 32-bit elements; how exact they have to be, the bound alone decides.
A program may use at most 128 MiB of HBM per device.

v0:
```python
import functools

import jax
import jax.numpy as jnp
from jax import lax
from jax.experimental import pallas as pl
from jax.experimental.pallas import tpu as pltpu
from jax.sharding import PartitionSpec as P

coupling = 0.5
mass_square = -1.0
step_size = 0.15

ROWS = 4
SPLIT = 2


def holder_row(replica):
    return replica // 4


def as_int(flag):
    return jnp.where(flag, 1, 0).astype(jnp.int32)


def line_items(wanted, at, passes, upward):
    items = [jnp.int32(-1)] * passes
    order = range(ROWS - 1, -1, -1) if upward else range(ROWS)
    seen, count = [], jnp.int32(0)
    for dest in order:
        name = wanted[dest]
        row = holder_row(name)
        active = as_int(name >= 0)
        if upward:
            active = active * as_int(dest > at) * as_int(row <= at)
        else:
            active = active * as_int(dest < at) * as_int(row >= at)
        for other in seen:
            active = active * as_int(other != name)
        for p in range(passes):
            items[p] = jnp.where(active * as_int(count == p) == 1, name, items[p])
        count = count + active
        seen.append(name)
    return items


def cross_items(wanted, first, passes):
    need = []
    for local in range(2):
        flag = jnp.int32(0)
        for dest in range(ROWS):
            flag = jnp.maximum(flag, as_int(wanted[dest] == first + local))
        need.append(flag)
    items = [jnp.where(need[0] == 1, first, jnp.where(need[1] == 1, first + 1, -1))]
    if passes > 1:
        items.append(jnp.where(need[0] * need[1] == 1, first + 1, -1))
    return items


def wishes(parent_ref):
    names, slots = [], []
    for group in range(2 * ROWS):
        first, second = parent_ref[2 * group], parent_ref[2 * group + 1]
        names.append(jnp.where(first != 2 * group, first, jnp.where(second != 2 * group + 1, second, -1)))
        slots.append(as_int(second != 2 * group + 1))
    return names, slots


def plan_kernel(parent_ref, out_ref):
    names, _ = wishes(parent_ref)
    most = jnp.int32(1)
    for column in range(2):
        wanted = [names[2 * row + column] for row in range(ROWS)]
        for row in range(ROWS):
            carried = [cross_items(wanted, jnp.int32(4 * row + 2 - 2 * column), 2)]
            carried += [line_items(wanted, row, ROWS - 1, upward) for upward in (True, False)]
            for items in carried:
                for p, item in enumerate(items):
                    most = jnp.where(item >= 0, jnp.maximum(most, p + 1), most)
    out_ref[0] = most


def links_needed(parent):
    smem = pl.BlockSpec(memory_space=pltpu.SMEM)
    return pl.pallas_call(
        plan_kernel, out_shape=jax.ShapeDtypeStruct((1,), jnp.int32), in_specs=[smem], out_specs=smem)(parent)[0]


def pick(name, candidates):
    value = candidates[0][1]
    for other, block in candidates[1:]:
        value = jnp.where(other == name, block, value)
    return value


def force(lower, center, upper):
    top = pltpu.roll(center, center.shape[0] - 1, 0)
    bottom = pltpu.roll(center, 1, 0)
    right = pltpu.roll(center, center.shape[1] - 1, 1)
    left = pltpu.roll(center, 1, 1)
    nearby = (lower + upper) + (top + bottom) + (right + left)
    value = nearby - center * ((6.0 + mass_square) + coupling * (center * center))
    return value, top, right


def action(center, upper, top, right):
    dz, dx, dy = upper - center, top - center, right - center
    square = center * center
    local = 0.5 * (dz * dz + dx * dx + dy * dy)
    local = local + square * (0.5 * mass_square + (0.25 * coupling) * square)
    return jnp.sum(local.reshape(local.shape[0] // 8, 8, local.shape[1]), axis=0)


def kernel(passes, slabs, delay, volume,
           parent_ref, field_ref, mom_ref, out_f, out_m, out_a,
           own, moved, mom, kick, mid, kick_b, end, rest_f, rest_m, res_f, res_m, sums, tiles, tiles_in,
           y_out, y_in, up_out, up_in, dn_out, dn_in,
           load_sem, store_sem, halo_s, halo_r, y_s, y_r, up_s, up_r, dn_s, dn_r, act_s, act_r):
    depth, wx, wy = field_ref.shape[1:]
    chunks = depth * SPLIT
    part = wx // SPLIT
    cross = min(passes, 2)
    rep = lax.axis_index("rep")
    slab = lax.axis_index("slab")
    z = rep // 2
    y = rep % 2
    partner = rep + 1 - 2 * y
    above = lax.rem(slab + 1, slabs)
    below = lax.rem(slab + slabs - 1, slabs)

    loads = [
        pltpu.make_async_copy(field_ref, own.at[:, 3:3 + depth], load_sem.at[0]),
        pltpu.make_async_copy(mom_ref, mom.at[:, 2:2 + depth], load_sem.at[1]),
    ]
    for copy in loads:
        copy.start()

    barrier = pltpu.get_barrier_semaphore()

    def greet(device):
        pl.semaphore_signal(barrier, inc=1, device_id=device, device_id_type=pl.DeviceIdType.MESH)

    for far in range(1, slabs):
        greet((rep, lax.rem(slab + far, slabs)))
    greet((partner, slab))

    @pl.when(z > 0)
    def _():
        greet((rep - 2, slab))

    @pl.when(z < ROWS - 1)
    def _():
        greet((rep + 2, slab))

    pl.semaphore_wait(barrier, slabs + as_int(z > 0) + as_int(z < ROWS - 1))

    def remote(src, dst, send, recv, device):
        return pltpu.make_async_remote_copy(
            src_ref=src, dst_ref=dst, send_sem=send, recv_sem=recv,
            device_id=device, device_id_type=pl.DeviceIdType.MESH)

    halos = [
        remote(field_ref.at[:, depth - 3:depth], own.at[:, 0:3], halo_s.at[0], halo_r.at[0], (rep, above)),
        remote(field_ref.at[:, 0:3], own.at[:, depth + 3:depth + 6], halo_s.at[1], halo_r.at[1], (rep, below)),
        remote(mom_ref.at[:, depth - 2:depth], mom.at[:, 0:2], halo_s.at[2], halo_r.at[2], (rep, above)),
        remote(mom_ref.at[:, 0:2], mom.at[:, depth + 2:depth + 4], halo_s.at[3], halo_r.at[3], (rep, below)),
    ]
    for copy in halos:
        copy.start()
    moved_halos = [
        remote(moved.at[depth:depth + 3], moved.at[0:3], halo_s.at[4], halo_r.at[4], (rep, above)),
        remote(moved.at[3:6], moved.at[depth + 3:depth + 6], halo_s.at[5], halo_r.at[5], (rep, below)),
    ]

    by_group, slots = wishes(parent_ref)
    mine, other = [], []
    for row in range(ROWS):
        mine.append(jnp.where(y == 0, by_group[2 * row], by_group[2 * row + 1]))
        other.append(jnp.where(y == 0, by_group[2 * row + 1], by_group[2 * row]))
    here, slot = jnp.int32(-1), jnp.int32(0)
    for group in range(2 * ROWS):
        here = jnp.where(rep == group, by_group[group], here)
        slot = jnp.where(rep == group, slots[group], slot)
    here = jnp.where(here >= 0, here, 2 * rep)
    y_out_items = cross_items(other, 2 * rep, cross)
    y_in_items = cross_items(mine, 2 * partner, cross)
    up_out_items = line_items(mine, z, passes, True)
    up_in_items = line_items(mine, z - 1, passes, True)
    dn_out_items = line_items(mine, z, passes, False)
    dn_in_items = line_items(mine, z + 1, passes, False)

    def copy_y(c):
        return remote(y_out.at[c], y_in.at[c], y_s.at[c], y_r.at[c], (partner, slab))

    def copy_up(c):
        return remote(up_out.at[c], up_in.at[c], up_s.at[c], up_r.at[c], (rep + 2, slab))

    def copy_dn(c):
        return remote(dn_out.at[c], dn_in.at[c], dn_s.at[c], dn_r.at[c], (rep - 2, slab))

    def layer_of(c):
        k = c // SPLIT
        return jnp.where(k < 3, k, jnp.where(k < 6, k + depth - 6, k - 3))

    def rows_of(c):
        return pl.ds(pl.multiple_of((c % SPLIT) * part, part), part)

    def own_blocks(c):
        layer, rows = layer_of(c), rows_of(c)
        return [(2 * rep, own[0, 3 + layer, rows]), (2 * rep + 1, own[1, 3 + layer, rows])]

    def cross_blocks(c):
        return [(y_in_items[q], y_in[c, q]) for q in range(cross)]

    def up_blocks(c):
        return [(up_in_items[q], up_in[c, q]) for q in range(passes)]

    def dn_blocks(c):
        return [(dn_in_items[q], dn_in[c, q]) for q in range(passes)]

    def layer_step(k, field_at, mom_at, counted, emit):
        k1, k2, k3 = k - 1, jnp.maximum(k - 2, 0), jnp.maximum(k - 3, 0)
        lower, center, upper = field_at(k - 1), field_at(k), field_at(k + 1)
        before, push = mom_at(k - 1), kick[k1]
        mid_low, mid_at = mid[k2], mid[k1]
        end_low, end_at, push_b = end[k3], end[k2], kick_b[k2]
        value, top, right = force(lower, center, upper)
        first = before + (0.5 * step_size) * value
        mid_up = center + step_size * first
        value, _, _ = force(mid_low, mid_at, mid_up)
        second = push + step_size * value
        end_up = mid_at + step_size * second
        value, _, _ = force(end_low, end_at, end_up)
        third = push_b + (0.5 * step_size) * value
        if counted:
            share = action(center, upper, top, right)
            sums[0] += jnp.where((k >= 3) & (k < depth + 3), share, 0.0)
        kick[k] = first
        mid[k] = mid_up
        kick_b[k1] = second
        end[k1] = end_up
        emit(jnp.maximum(k - 5, 0), end_at, third)

    def moved_action(k):
        center, upper = moved[k], moved[k + 1]
        top = pltpu.roll(center, wx - 1, 0)
        right = pltpu.roll(center, wy - 1, 1)
        sums[1] += action(center, upper, top, right)

    sums[...] = jnp.zeros_like(sums)
    loads[0].wait()
    rest = 1 - slot
    steps = depth + 4
    total = chunks + ROWS * delay
    begin_rest = total - steps
    up_skew = delay * (z + 1)
    dn_skew = delay * (ROWS - z)
    end_skew = jnp.maximum(up_skew, dn_skew)

    def rest_emit(layer, field, momentum):
        rest_f[layer] = field
        rest_m[layer] = momentum

    def during(t, skew):
        return (t >= skew) & (t < skew + chunks)

    def step(t, _):
        @pl.when(t < chunks)
        def _():
            blocks = own_blocks(t)
            for p in range(cross):
                y_out[t, p] = pick(y_out_items[p], blocks)
            copy_y(t).start()

        @pl.when(during(t, delay))
        def _():
            copy_y(t - delay).wait_recv()

        @pl.when(during(t, up_skew) & (z > 0))
        def _():
            copy_up(t - up_skew).wait_recv()

        @pl.when(during(t, dn_skew) & (z < ROWS - 1))
        def _():
            copy_dn(t - dn_skew).wait_recv()

        @pl.when(during(t, up_skew) & (z < ROWS - 1))
        def _():
            c = t - up_skew
            blocks = own_blocks(c) + cross_blocks(c) + up_blocks(c)
            for p in range(passes):
                up_out[c, p] = pick(up_out_items[p], blocks)
            copy_up(c).start()

        @pl.when(during(t, dn_skew) & (z > 0))
        def _():
            c = t - dn_skew
            blocks = own_blocks(c) + cross_blocks(c) + dn_blocks(c)
            for p in range(passes):
                dn_out[c, p] = pick(dn_out_items[p], blocks)
            copy_dn(c).start()

        @pl.when(during(t, end_skew))
        def _():
            c = t - end_skew
            blocks = own_blocks(c) + cross_blocks(c) + up_blocks(c) + dn_blocks(c)
            moved[3 + layer_of(c), rows_of(c)] = pick(here, blocks)

            @pl.when((c >= 6 * SPLIT) & (c % SPLIT == SPLIT - 1))
            def _():
                moved_action(c // SPLIT - 1)

        @pl.when(t == end_skew + 6 * SPLIT - 1)
        def _():
            for copy in moved_halos:
                copy.start()

        @pl.when(t == begin_rest)
        def _():
            loads[1].wait()
            for copy in halos:
                copy.wait_recv()

        @pl.when(t >= begin_rest)
        def _():
            layer_step(t - begin_rest + 1, lambda k: own[rest, k], lambda k: mom[rest, k], True, rest_emit)

        return 0

    lax.fori_loop(0, total, step, 0)
    for copy in moved_halos:
        copy.wait_recv()

    def rest_of_action(i, _):
        moved_action(jnp.where(i < 2, i + 3, i + depth - 3))
        return 0

    lax.fori_loop(0, 6, rest_of_action, 0)
    tiles[0] = jnp.where(slot == 0, sums[1], sums[0])
    tiles[1] = jnp.where(slot == 0, sums[0], sums[1])
    shares = [
        remote(tiles, tiles_in.at[far - 1], act_s.at[far - 1], act_r.at[far - 1],
               (rep, lax.rem(slab + far, slabs)))
        for far in range(1, slabs)
    ]
    for copy in shares:
        copy.start()

    def moved_emit(layer, field, momentum):
        other_f, other_m = rest_f[layer], rest_m[layer]
        res_f[0, layer] = jnp.where(slot == 0, field, other_f)
        res_f[1, layer] = jnp.where(slot == 0, other_f, field)
        res_m[0, layer] = jnp.where(slot == 0, momentum, other_m)
        res_m[1, layer] = jnp.where(slot == 0, other_m, momentum)

    group = depth // 4

    def stores(i):
        layers = pl.ds(i * group, group)
        return [
            pltpu.make_async_copy(res_f.at[:, layers], out_f.at[:, layers], store_sem.at[0, i]),
            pltpu.make_async_copy(res_m.at[:, layers], out_m.at[:, layers], store_sem.at[1, i]),
        ]

    def moved_step(k, _):
        layer_step(k, lambda i: moved[i], lambda i: mom[slot, i], False, moved_emit)

        @pl.when((k >= group + 4) & ((k - 4) % group == 0))
        def _():
            for copy in stores((k - 4) // group - 1):
                copy.start()

        return 0

    lax.fori_loop(1, steps + 1, moved_step, 0)

    for copy in halos + moved_halos:
        copy.wait_send()

    def drain(c, _):
        copy_y(c).wait_send()

        @pl.when(z < ROWS - 1)
        def _():
            copy_up(c).wait_send()

        @pl.when(z > 0)
        def _():
            copy_dn(c).wait_send()

        return 0

    lax.fori_loop(0, chunks, drain, 0)
    for i in range(4):
        for copy in stores(i):
            copy.wait()
    for copy in shares:
        copy.wait()
    whole = tiles[...]
    for far in range(1, slabs):
        whole = whole + tiles_in[far - 1]
    out_a[0] = jnp.sum(whole[0]) * (1.0 / volume)
    out_a[1] = jnp.sum(whole[1]) * (1.0 / volume)


def run(passes, slabs, delay, replica_field, momentum, parent):
    pair, depth, wx, wy = replica_field.shape
    chunks = depth * SPLIT
    part = wx // SPLIT
    cross = min(passes, 2)
    f32 = jnp.float32

    def plane(*lead):
        return pltpu.VMEM((*lead, wx, wy), f32)

    def block(count):
        return pltpu.VMEM((chunks, count, part, wy), f32)

    dma = pltpu.SemaphoreType.DMA
    volume = depth * slabs * wx * wy
    return pl.pallas_call(
        functools.partial(kernel, passes, slabs, delay, volume),
        out_shape=(
            jax.ShapeDtypeStruct(replica_field.shape, f32),
            jax.ShapeDtypeStruct(replica_field.shape, f32),
            jax.ShapeDtypeStruct((pair,), f32),
        ),
        in_specs=[
            pl.BlockSpec(memory_space=pltpu.SMEM),
            pl.BlockSpec(memory_space=pl.ANY),
            pl.BlockSpec(memory_space=pl.ANY),
        ],
        out_specs=(
            pl.BlockSpec(memory_space=pl.ANY),
            pl.BlockSpec(memory_space=pl.ANY),
            pl.BlockSpec(memory_space=pltpu.SMEM),
        ),
        scratch_shapes=[
            plane(pair, depth + 6), plane(depth + 6), plane(pair, depth + 4),
            plane(depth + 6), plane(depth + 6), plane(depth + 6), plane(depth + 6),
            plane(depth), plane(depth), plane(pair, depth), plane(pair, depth),
            pltpu.VMEM((2, 8, wy), f32), pltpu.VMEM((2, 8, wy), f32), pltpu.VMEM((slabs - 1, 2, 8, wy), f32),
            block(cross), block(cross), block(passes), block(passes), block(passes), block(passes),
            dma((2,)), dma((2, 4)), dma((6,)), dma((6,)),
            dma((chunks,)), dma((chunks,)), dma((chunks,)), dma((chunks,)), dma((chunks,)), dma((chunks,)),
            dma((slabs - 1,)), dma((slabs - 1,)),
        ],
        compiler_params=pltpu.CompilerParams(
            collective_id=passes, has_side_effects=True, vmem_limit_bytes=56 * 2**20),
    )(parent, replica_field, momentum)


def routed(replica_field, momentum, parent):
    slabs = lax.axis_size("slab")
    branches = [functools.partial(run, passes, slabs, delay) for passes, delay in ((1, 5), (2, 3), (3, 2))]
    return lax.switch(links_needed(parent) - 1, branches, replica_field, momentum, parent)


def padded(shard, sides, width):
    for axis, dim in sides:
        devices, length = (lax.axis_size(axis), shard.shape[dim])
        up = [(i, (i + 1) % devices) for i in range(devices)]
        down = [(j, i) for i, j in up]
        last = lax.slice_in_dim(shard, length - width, length, axis=dim)
        initial = lax.slice_in_dim(shard, 0, width, axis=dim)
        before = lax.ppermute(last, axis, up)
        after = lax.ppermute(initial, axis, down)
        shard = jnp.concatenate([before, shard, after], axis=dim)
    return shard


def force_inner(extended):
    center = extended[:, 1:-1]
    nearby = extended[:, :-2] + extended[:, 2:]
    nearby = nearby + jnp.roll(center, 1, 2) + jnp.roll(center, -1, 2)
    nearby = nearby + jnp.roll(center, 1, 3) + jnp.roll(center, -1, 3)
    return nearby - 6.0 * center - mass_square * center - coupling * center * center * center


def action_inner(extended):
    center = extended[:, 1:-1]
    along_z = extended[:, 2:] - center
    along_x = jnp.roll(center, -1, 2) - center
    along_y = jnp.roll(center, -1, 3) - center
    local = 0.5 * (along_z * along_z + along_x * along_x + along_y * along_y)
    local = (
        local
        + 0.5 * mass_square * center * center
        + 0.25 * coupling * center * center * center * center
    )
    return jnp.sum(local, axis=(1, 2, 3))


def extend_one(values):
    return padded(values, (("slab", 1),), 1)


def shards(replica_field, momentum, parent):
    per_group = replica_field.shape[0]
    depth = replica_field.shape[1]
    width_x = replica_field.shape[2]
    width_y = replica_field.shape[3]
    flat = replica_field.reshape(per_group, depth, width_x * width_y)
    spread = lax.all_to_all(flat, "rep", split_axis=2, concat_axis=0, tiled=True)
    copied = jnp.take(spread, parent, axis=0)
    returned = lax.all_to_all(copied, "rep", split_axis=0, concat_axis=2, tiled=True)
    field_start = returned.reshape(per_group, depth, width_x, width_y)
    volume = depth * lax.axis_size("slab") * width_x * width_y
    extended = extend_one(field_start)
    partial_action = action_inner(extended)
    half_kick = momentum + 0.5 * step_size * force_inner(extended)
    field_mid = field_start + step_size * half_kick
    kicked = half_kick + step_size * force_inner(extend_one(field_mid))
    field_end = field_mid + step_size * kicked
    momentum_end = kicked + 0.5 * step_size * force_inner(extend_one(field_end))
    density = lax.psum(partial_action, "slab") / volume
    return (field_end, momentum_end, density)


def solution(mesh):
    in_specs = (P("rep", "slab", None, None), P("rep", "slab", None, None), P())
    out_specs = (P("rep", "slab", None, None), P("rep", "slab", None, None), P("rep"))
    plan = routed if mesh.shape["rep"] == 2 * ROWS and mesh.shape["slab"] > 2 else shards
    return jax.shard_map(plan, mesh=mesh, in_specs=in_specs, out_specs=out_specs, check_vma=False)
```

profile of v0, /device:TPU:0, one launch (start us, length us, event | category | flops | bytes accessed | tf_op | source)
XLA Modules:
  0.0 54.5 jit_solution(17305027942063637547)
XLA Ops:
  0.6 1.5 %shard_map.73 = s32[1]{0:T(128)} custom-call(s32[16]{0:T(128)} %parent_ref.1), custom_call_target="tpu_custom_call" | custom-call | tf_op jit(solution)/shard_map/pallas_call | solution.py:85
  2.8 47.5 %conditional.1 = ((f32[2,16,128,128]{3,2,1,0:T(8,128)S(1)}, f32[2,16,128,128]{3,2,1,0:T(8,128)}, f32[2]{0:T(128)S(1)})) conditional(s32[]{:T(128)} %bitcast, (s32[16]{0:T(128)}, f32[2,16,128,128]{3,2,1,0:T(8,128)}, f32[2,16,128,128]{3,2,1,0:T(8,128)}) %tuple.16, (s32[16]{0:T(128)}, f32[2,16,128,128]{3,2,1,0:T(8,128)}, ...), branch_computations={%region_0.0_spmd, %region_1.0_spmd, %region_2.0_spmd} | conditional | bytes 8 | solution.py:456
  2.8 47.5 %branch_0_fun.1 = (f32[2,16,128,128]{3,2,1,0:T(8,128)S(1)}, f32[2,16,128,128]{3,2,1,0:T(8,128)}, f32[2]{0:T(128)S(1)}) custom-call(s32[16]{0:T(128)} %get-tuple-element.18.parent_ref, f32[2,16,128,128]{3,2,1,0:T(8,128)} %get-tuple-element.48.field_ref, f32[2,16,128,128]{3,2,1,0:T(8,128)} %get-tuple-element.51.mom_ref), custom_call_target="tpu_custom_call" | custom-call | tf_op jit(solution)/shard_map/cond/branch_0_fun/pallas_call | solution.py:421
  50.3 0.0 copy-start
  50.3 1.3 %copy.33 = f32[2,16,128,128]{3,2,1,0:T(8,128)} copy(f32[2,16,128,128]{3,2,1,0:T(8,128)S(1)} %get-tuple-element.66) | data formatting | bytes 4194304
  51.6 1.0 %copy-done = f32[2,16,128,128]{3,2,1,0:T(8,128)S(1)} copy-done((f32[2,16,128,128]{3,2,1,0:T(8,128)S(1)}, f32[2,16,128,128]{3,2,1,0:T(8,128)}, u32[]{:S(2)}) %copy-start) | copy-done | bytes 2097176
  52.6 1.3 %copy.34 = f32[2,16,128,128]{3,2,1,0:T(8,128)} copy(f32[2,16,128,128]{3,2,1,0:T(8,128)S(1)} %copy-done) | data formatting | bytes 4194304
  54.0 0.5 copy.35
Async XLA Ops:
  50.3 2.3 %copy-start = (f32[2,16,128,128]{3,2,1,0:T(8,128)S(1)}, f32[2,16,128,128]{3,2,1,0:T(8,128)}, u32[]{:S(2)}) copy-start(f32[2,16,128,128]{3,2,1,0:T(8,128)} %get-tuple-element.67) | copy-start | bytes 6291460
where the time goes:
time: 54.7 us; the launch traced here: 54.5 us
  Pallas kernels  49 us (90%)
  local copies, waits for them, and re-layouts  4.17 us (8%)
  between operations  1.3 us (2%)
    pallas_call x1, Pallas kernels, run(): pl.pallas_call(functools.partial(kernel, passes, slabs, delay, volume), o...  47.5 us
    unnamed x5, local copies, waits for them, and re-layouts  4.17 us
    pallas_call x1, Pallas kernels, links_needed(): pl.pallas_call(plan_kernel, out_shape=jax.ShapeDtypeStruct((1,), jnp.int3...  1.49 us

commit v1 on v0

--- a/solution.py
+++ b/solution.py
@@ -19,16 +19,18 @@
     return replica // 4
 
 
+def holder_column(replica):
+    return (replica // 2) % 2
+
+
 def as_int(flag):
     return jnp.where(flag, 1, 0).astype(jnp.int32)
 
 
 def line_items(wanted, at, passes, upward):
     items = [jnp.int32(-1)] * passes
-    order = range(ROWS - 1, -1, -1) if upward else range(ROWS)
     seen, count = [], jnp.int32(0)
-    for dest in order:
-        name = wanted[dest]
+    for dest, name in sorted(wanted, key=lambda pair: -pair[0] if upward else pair[0]):
         row = holder_row(name)
         active = as_int(name >= 0)
         if upward:
@@ -44,6 +46,10 @@
     return items
 
 
+def held_in(names, column):
+    return [(group // 2, jnp.where(holder_column(name) == column, name, -1)) for group, name in enumerate(names)]
+
+
 def cross_items(wanted, first, passes):
     need = []
     for local in range(2):
@@ -68,19 +74,24 @@
 
 def plan_kernel(parent_ref, out_ref):
     names, _ = wishes(parent_ref)
-    most = jnp.int32(1)
+    y_first, z_first = jnp.int32(1), jnp.int32(1)
     for column in range(2):
         wanted = [names[2 * row + column] for row in range(ROWS)]
+        by_row = list(enumerate(wanted))
+        held = held_in(names, column)
         for row in range(ROWS):
             carried = [cross_items(wanted, jnp.int32(4 * row + 2 - 2 * column), 2)]
-            carried += [line_items(wanted, row, ROWS - 1, upward) for upward in (True, False)]
+            carried += [line_items(by_row, row, ROWS - 1, upward) for upward in (True, False)]
             for items in carried:
                 for p, item in enumerate(items):
-                    most = jnp.where(item >= 0, jnp.maximum(most, p + 1), most)
-    out_ref[0] = most
-
-
-def links_needed(parent):
+                    y_first = jnp.where(item >= 0, jnp.maximum(y_first, p + 1), y_first)
+            for upward in (True, False):
+                for p, item in enumerate(line_items(held, row, 2, upward)):
+                    z_first = jnp.where(item >= 0, jnp.maximum(z_first, p + 1), z_first)
+    out_ref[0] = jnp.where(y_first == 1, 0, jnp.where(z_first == 1, 1, y_first))
+
+
+def plan_for(parent):
     smem = pl.BlockSpec(memory_space=pltpu.SMEM)
     return pl.pallas_call(
         plan_kernel, out_shape=jax.ShapeDtypeStruct((1,), jnp.int32), in_specs=[smem], out_specs=smem)(parent)[0]
@@ -111,7 +122,7 @@
     return jnp.sum(local.reshape(local.shape[0] // 8, 8, local.shape[1]), axis=0)
 
 
-def kernel(passes, slabs, delay, volume,
+def kernel(passes, y_first, slabs, delay, volume,
            parent_ref, field_ref, mom_ref, out_f, out_m, out_a,
            own, moved, mom, kick, mid, kick_b, end, rest_f, rest_m, res_f, res_m, sums, tiles, tiles_in,
            y_out, y_in, up_out, up_in, dn_out, dn_in,
@@ -119,7 +130,7 @@
     depth, wx, wy = field_ref.shape[1:]
     chunks = depth * SPLIT
     part = wx // SPLIT
-    cross = min(passes, 2)
+    cross = min(passes, 2) if y_first else 1
     rep = lax.axis_index("rep")
     slab = lax.axis_index("slab")
     z = rep // 2
@@ -173,21 +184,26 @@
     ]
 
     by_group, slots = wishes(parent_ref)
-    mine, other = [], []
-    for row in range(ROWS):
-        mine.append(jnp.where(y == 0, by_group[2 * row], by_group[2 * row + 1]))
-        other.append(jnp.where(y == 0, by_group[2 * row + 1], by_group[2 * row]))
-    here, slot = jnp.int32(-1), jnp.int32(0)
+    here, there, slot = jnp.int32(-1), jnp.int32(-1), jnp.int32(0)
     for group in range(2 * ROWS):
         here = jnp.where(rep == group, by_group[group], here)
+        there = jnp.where(partner == group, by_group[group], there)
         slot = jnp.where(rep == group, slots[group], slot)
+    if y_first:
+        mine = [jnp.where(y == 0, by_group[2 * row], by_group[2 * row + 1]) for row in range(ROWS)]
+        other = [jnp.where(y == 0, by_group[2 * row + 1], by_group[2 * row]) for row in range(ROWS)]
+        y_out_items = cross_items(other, 2 * rep, cross)
+        y_in_items = cross_items(mine, 2 * partner, cross)
+        wanted = list(enumerate(mine))
+    else:
+        y_out_items = [jnp.where(holder_column(there) == y, there, -1)]
+        y_in_items = [jnp.where(holder_column(here) == y, -1, here)]
+        wanted = held_in(by_group, y)
     here = jnp.where(here >= 0, here, 2 * rep)
-    y_out_items = cross_items(other, 2 * rep, cross)
-    y_in_items = cross_items(mine, 2 * partner, cross)
-    up_out_items = line_items(mine, z, passes, True)
-    up_in_items = line_items(mine, z - 1, passes, True)
-    dn_out_items = line_items(mine, z, passes, False)
-    dn_in_items = line_items(mine, z + 1, passes, False)
+    up_out_items = line_items(wanted, z, passes, True)
+    up_in_items = line_items(wanted, z - 1, passes, True)
+    dn_out_items = line_items(wanted, z, passes, False)
+    dn_in_items = line_items(wanted, z + 1, passes, False)
 
     def copy_y(c):
         return remote(y_out.at[c], y_in.at[c], y_s.at[c], y_r.at[c], (partner, slab))
@@ -253,9 +269,12 @@
     steps = depth + 4
     total = chunks + ROWS * delay
     begin_rest = total - steps
-    up_skew = delay * (z + 1)
-    dn_skew = delay * (ROWS - z)
-    end_skew = jnp.maximum(up_skew, dn_skew)
+    farther = jnp.maximum(z, ROWS - 1 - z)
+    end_skew = delay * (farther + 1)
+    if y_first:
+        y_skew, y_wait, up_skew, dn_skew = 0, delay, delay * (z + 1), delay * (ROWS - z)
+    else:
+        y_skew, y_wait, up_skew, dn_skew = delay * farther, end_skew, delay * z, delay * (ROWS - 1 - z)
 
     def rest_emit(layer, field, momentum):
         rest_f[layer] = field
@@ -265,29 +284,30 @@
         return (t >= skew) & (t < skew + chunks)
 
     def step(t, _):
-        @pl.when(t < chunks)
-        def _():
-            blocks = own_blocks(t)
+        @pl.when(during(t, y_wait))
+        def _():
+            copy_y(t - y_wait).wait_recv()
+
+        @pl.when(during(t, up_skew) & (z > 0))
+        def _():
+            copy_up(t - up_skew).wait_recv()
+
+        @pl.when(during(t, dn_skew) & (z < ROWS - 1))
+        def _():
+            copy_dn(t - dn_skew).wait_recv()
+
+        @pl.when(during(t, y_skew))
+        def _():
+            c = t - y_skew
+            blocks = own_blocks(c) + ([] if y_first else up_blocks(c) + dn_blocks(c))
             for p in range(cross):
-                y_out[t, p] = pick(y_out_items[p], blocks)
-            copy_y(t).start()
-
-        @pl.when(during(t, delay))
-        def _():
-            copy_y(t - delay).wait_recv()
-
-        @pl.when(during(t, up_skew) & (z > 0))
-        def _():
-            copy_up(t - up_skew).wait_recv()
-
-        @pl.when(during(t, dn_skew) & (z < ROWS - 1))
-        def _():
-            copy_dn(t - dn_skew).wait_recv()
+                y_out[c, p] = pick(y_out_items[p], blocks)
+            copy_y(c).start()
 
         @pl.when(during(t, up_skew) & (z < ROWS - 1))
         def _():
             c = t - up_skew
-            blocks = own_blocks(c) + cross_blocks(c) + up_blocks(c)
+            blocks = own_blocks(c) + (cross_blocks(c) if y_first else []) + up_blocks(c)
             for p in range(passes):
                 up_out[c, p] = pick(up_out_items[p], blocks)
             copy_up(c).start()
@@ -295,7 +315,7 @@
         @pl.when(during(t, dn_skew) & (z > 0))
         def _():
             c = t - dn_skew
-            blocks = own_blocks(c) + cross_blocks(c) + dn_blocks(c)
+            blocks = own_blocks(c) + (cross_blocks(c) if y_first else []) + dn_blocks(c)
             for p in range(passes):
                 dn_out[c, p] = pick(dn_out_items[p], blocks)
             copy_dn(c).start()
@@ -403,11 +423,11 @@
     out_a[1] = jnp.sum(whole[1]) * (1.0 / volume)
 
 
-def run(passes, slabs, delay, replica_field, momentum, parent):
+def run(passes, y_first, slabs, delay, replica_field, momentum, parent):
     pair, depth, wx, wy = replica_field.shape
     chunks = depth * SPLIT
     part = wx // SPLIT
-    cross = min(passes, 2)
+    cross = min(passes, 2) if y_first else 1
     f32 = jnp.float32
 
     def plane(*lead):
@@ -419,7 +439,7 @@
     dma = pltpu.SemaphoreType.DMA
     volume = depth * slabs * wx * wy
     return pl.pallas_call(
-        functools.partial(kernel, passes, slabs, delay, volume),
+        functools.partial(kernel, passes, y_first, slabs, delay, volume),
         out_shape=(
             jax.ShapeDtypeStruct(replica_field.shape, f32),
             jax.ShapeDtypeStruct(replica_field.shape, f32),
@@ -446,14 +466,15 @@
             dma((slabs - 1,)), dma((slabs - 1,)),
         ],
         compiler_params=pltpu.CompilerParams(
-            collective_id=passes, has_side_effects=True, vmem_limit_bytes=56 * 2**20),
+            collective_id=passes + (0 if y_first else ROWS), has_side_effects=True, vmem_limit_bytes=56 * 2**20),
     )(parent, replica_field, momentum)
 
 
 def routed(replica_field, momentum, parent):
     slabs = lax.axis_size("slab")
-    branches = [functools.partial(run, passes, slabs, delay) for passes, delay in ((1, 5), (2, 3), (3, 2))]
-    return lax.switch(links_needed(parent) - 1, branches, replica_field, momentum, parent)
+    plans = ((1, True, 5), (1, False, 5), (2, True, 3), (3, True, 2))
+    branches = [functools.partial(run, passes, y_first, slabs, delay) for passes, y_first, delay in plans]
+    return lax.switch(plan_for(parent), branches, replica_field, momentum, parent)
 
 
 def padded(shard, sides, width):

time: 54.7 us -> 55.4 us (1.013)
  Pallas kernels: 49 us -> 49.7 us
    pallas_call x2, Pallas kernels: 49 us -> 49.7 us  [the longest x1 47.8 us: run(): pl.pallas_call(functools.partial(kernel, passes, y_first, slabs, delay, v...]
where the time goes in v1:
time: 55.4 us; the launch traced here: 55.2 us
  Pallas kernels  49.7 us (90%)
  local copies, waits for them, and re-layouts  4.17 us (8%)
  between operations  1.3 us (2%)
    pallas_call x1, Pallas kernels, run(): pl.pallas_call(functools.partial(kernel, passes, y_first, slabs, delay, v...  47.8 us
    unnamed x5, local copies, waits for them, and re-layouts  4.17 us
    pallas_call x1, Pallas kernels, plan_for(): pl.pallas_call(plan_kernel, out_shape=jax.ShapeDtypeStruct((1,), jnp.int3...  1.98 us

profile of v1, /device:TPU:0, one launch (start us, length us, event | category | flops | bytes accessed | tf_op | source)
XLA Modules:
  0.0 55.2 jit_solution(12295500321609528884)
XLA Ops:
  0.6 2.0 %shard_map.78 = s32[1]{0:T(128)} custom-call(s32[16]{0:T(128)} %parent_ref.1), custom_call_target="tpu_custom_call" | custom-call | tf_op jit(solution)/shard_map/pallas_call | solution.py:96
  3.3 47.8 %conditional.1 = ((f32[2,16,128,128]{3,2,1,0:T(8,128)S(1)}, f32[2,16,128,128]{3,2,1,0:T(8,128)}, f32[2]{0:T(128)S(1)})) conditional(s32[]{:T(128)} %bitcast, (s32[16]{0:T(128)}, f32[2,16,128,128]{3,2,1,0:T(8,128)}, f32[2,16,128,128]{3,2,1,0:T(8,128)}) %tuple.19, (s32[16]{0:T(128)}, f32[2,16,128,128]{3,2,1,0:T(8,128)}, ...), branch_computations={%region_0.0_spmd, %region_1.0_spmd, %region_2.0_spmd, %region_3.0_... | conditional | bytes 8 | solution.py:477
  3.3 47.8 %branch_1_fun.1 = (f32[2,16,128,128]{3,2,1,0:T(8,128)S(1)}, f32[2,16,128,128]{3,2,1,0:T(8,128)}, f32[2]{0:T(128)S(1)}) custom-call(s32[16]{0:T(128)} %get-tuple-element.27.parent_ref, f32[2,16,128,128]{3,2,1,0:T(8,128)} %get-tuple-element.63.field_ref, f32[2,16,128,128]{3,2,1,0:T(8,128)} %get-tuple-element.67.mom_ref), custom_call_target="tpu_custom_call" | custom-call | tf_op jit(solution)/shard_map/cond/branch_1_fun/pallas_call | solution.py:441
  51.1 0.0 copy-start
  51.1 1.3 %copy.41 = f32[2,16,128,128]{3,2,1,0:T(8,128)} copy(f32[2,16,128,128]{3,2,1,0:T(8,128)S(1)} %get-tuple-element.85) | data formatting | bytes 4194304
  52.4 1.0 %copy-done = f32[2,16,128,128]{3,2,1,0:T(8,128)S(1)} copy-done((f32[2,16,128,128]{3,2,1,0:T(8,128)S(1)}, f32[2,16,128,128]{3,2,1,0:T(8,128)}, u32[]{:S(2)}) %copy-start) | copy-done | bytes 2097176
  53.4 1.3 %copy.42 = f32[2,16,128,128]{3,2,1,0:T(8,128)} copy(f32[2,16,128,128]{3,2,1,0:T(8,128)S(1)} %copy-done) | data formatting | bytes 4194304
  54.7 0.5 copy.43
Async XLA Ops:
  51.1 2.3 %copy-start = (f32[2,16,128,128]{3,2,1,0:T(8,128)S(1)}, f32[2,16,128,128]{3,2,1,0:T(8,128)}, u32[]{:S(2)}) copy-start(f32[2,16,128,128]{3,2,1,0:T(8,128)} %get-tuple-element.86) | copy-start | bytes 6291460
